TPU v7x, 32 devices: a whole 2x2x4 slice. The times are simulated.
32 devices in a mesh: groups: 2 (over x), chan: 16 (over z, y, core).
Axes of the slice: x: 2, y: 2, z: 4, core: 2. Of those that a mesh axis runs over, the one named last changes fastest.
Arguments:
- raw: bfloat16 [5120, 4096], P('chan', 'groups'), parts along dimension 1, may hold values from -50 to 50
- taps: bfloat16 [255], replicated, may hold values from -0.375 to 0.375
- tile_dist: int32 [16, 8], P('chan', 'groups'), parts along dimension 1, may hold values from 1 to 4, as said below
- tile_count: int32 [32], P(('groups', 'chan')), parts along dimension 0, may hold values from 0 to 4
- owner: int32 [8], P('groups'), parts along dimension 0, may hold values from 0 to 15, as said below
Outputs:
- band_stack: float32 [16, 256, 128], P('chan', 'groups'), parts along dimension 1
There are 2 independent parts, one for each index of `groups`. A program takes and returns all parts, laid end to end along the dimension named above; an argument that names none is the same for every part. Nothing has to cross between parts.
Inputs may be any that keep to these rules, and one draw needn't show every extreme that they name: Each row of tile_dist holds every distance of 1 to 4 once; in row i the first tile_count[i] entries d satisfy i + d < 16. `owner`: the owners are distinct, and some band is owned by index 15.
All inputs are finite; a program needn't handle non-finite values.
Results may differ from a plain program's by a relative error of at most 0.014.
Values may be sent and summed in bfloat16 or wider, within the bound.
A program may use at most 128 MiB of HBM per device.

v0:
```python
import math

import jax
import jax.numpy as jnp
from jax import lax
from jax.sharding import PartitionSpec as P


def extended(x, sides, width):
    for axis, dim in sides:
        size, length = (lax.axis_size(axis), x.shape[dim])
        up = [(i, (i + 1) % size) for i in range(size - 1)]
        down = [(j, i) for i, j in up]
        last = lax.slice_in_dim(x, length - width, length, axis=dim)
        initial = lax.slice_in_dim(x, 0, width, axis=dim)
        before = lax.ppermute(last, axis, up)
        after = lax.ppermute(initial, axis, down)
        x = jnp.concatenate([before, x, after], axis=dim)
    return x


def passed_along(x, axis, by):
    size = lax.axis_size(axis)
    pairs = [(i, i + by) for i in range(size) if 0 <= i + by < size]
    return lax.ppermute(x, axis, pairs)


def band_matrix(taps, out_rows, in_cols):
    width = taps.shape[0]
    offset = (
        jnp.arange(in_cols, dtype=jnp.int32)[None, :]
        - 5 * jnp.arange(out_rows, dtype=jnp.int32)[:, None]
    )
    inside = (offset >= 0) & (offset < width)
    picked = jnp.take(taps, jnp.clip(offset, 0, width - 1))
    return jnp.where(inside, picked, jnp.zeros_like(picked))


def whiten(block):
    length, channels = block.shape
    bins = length // 16
    freqs = jnp.arange(1, bins + 1, dtype=jnp.int32)[:, None]
    times = jnp.arange(length, dtype=jnp.int32)[None, :]
    angle = (freqs * times % length).astype(jnp.float32) * (2.0 * math.pi / length)
    table = jnp.concatenate([jnp.cos(angle), -jnp.sin(angle)], axis=0)
    table_high = table.astype(jnp.bfloat16)
    table_low = (table - table_high.astype(jnp.float32)).astype(jnp.bfloat16)
    spectrum = jnp.dot(table_high, block, preferred_element_type=jnp.float32)
    spectrum = spectrum + jnp.dot(table_low, block, preferred_element_type=jnp.float32)
    squares = spectrum * spectrum
    power = jnp.sum(squares[:bins] + squares[bins:], axis=1) / (2 * channels)
    gain = lax.rsqrt(power + 1e-06)
    return (spectrum * jnp.concatenate([gain, gain])[:, None]).astype(jnp.bfloat16)


def cross_tile(mine, partner, scale):
    product = lax.dot_general(
        mine, partner, (((0,), (0,)), ((), ())), preferred_element_type=jnp.float32
    )
    return product * scale


def shards(raw, taps, tile_dist, tile_count, owner):
    rows = raw.shape[0]
    width = taps.shape[0]
    half = (width - 1) // 2
    out_rows = rows // 5
    banded = band_matrix(taps, out_rows, rows + 2 * half)
    padded = extended(raw, (("chan", 0),), half)
    filtered = jnp.dot(banded, padded, preferred_element_type=jnp.float32)
    decimated = filtered.astype(jnp.bfloat16)
    regrouped = lax.all_to_all(decimated, "chan", split_axis=1, concat_axis=0, tiled=True)
    whitened = whiten(regrouped)
    channels = whitened.shape[1]
    scale = 1.0 / whitened.shape[0]
    bands = tile_dist.shape[1]
    slots = jnp.arange(bands, dtype=jnp.int32) < tile_count[0]
    partner = whitened
    stacks = []
    for distance in range(1, bands + 1):
        partner = passed_along(whitened, "chan", -distance)
        listed = jnp.sum(((tile_dist[0] == distance) & slots).astype(jnp.int32))
        tile = lax.cond(
            listed > 0,
            lambda first, second: cross_tile(first, second, scale),
            lambda first, second: jnp.zeros((channels, channels), jnp.float32),
            whitened,
            partner,
        )
        stacks.append(tile)
    stacked = jnp.stack(stacks)
    totals = lax.psum(stacked, "chan")
    selected = (owner == lax.axis_index("chan")).astype(jnp.float32)
    return jnp.einsum("b,bxy->xy", selected, totals, precision=lax.Precision.HIGHEST)[None]


def solution(mesh):
    in_specs = (P("chan", "groups"), P(), P("chan", "groups"), P(("groups", "chan")), P("groups"))
    out_specs = P("chan", "groups", None)
    return jax.shard_map(shards, mesh=mesh, in_specs=in_specs, out_specs=out_specs, check_vma=False)
```

profile of v0, /device:TPU:0, one launch (start us, length us, event | category | flops | bytes accessed | tf_op | source)
XLA Modules:
  0.0 350.4 jit_solution(16321516343890510298)
XLA Ops:
  6.5 0.0 copy-start
  6.5 1.3 fusion.63
  7.9 2.4 collective-permute-start
  10.3 1.3 collective-permute-start.1
  11.6 0.1 compare_select_fusion
  11.7 0.2 reshape.83
  11.9 0.0 copy-done
  12.0 0.0 copy-start.1
  12.0 202.9 %gather_fusion = bf16[36736]{0:T(1024)(128)(2,1)S(1)} fusion(bf16[255]{0:T(256)(128)(2,1)S(1)} %copy-done, s32[36864]{0:T(1024)S(1)} %pad_clamp_fusion), kind=kCustom, calls=%fused_computation | custom fusion | bytes 293888 | tf_op jit(solution)/shard_map/jit(_take)/gather | solution.py:35
  214.9 0.2 reshape.82
  215.1 0.0 collective-permute-done
  215.1 0.0 collective-permute-done.1
  215.1 0.0 copy-done.1
  215.1 1.9 fusion.13
  217.0 0.8 copy.13
  217.8 9.3 %all-to-all-start = ((bf16[64,16,128]{2,0,1:T(8,128)(2,1)}), bf16[64,16,128]{2,0,1:T(8,128)(2,1)S(1)}, u32[]{:S(2)}, u32[]{:S(2)}) async-start(bf16[64,16,128]{2,0,1:T(8,128)(2,1)} %bitcast.58), calls=%async_computation | async-start | bytes 524288 | tf_op jit(solution)/shard_map/all_to_all | solution.py:72
  227.1 0.0 copy-start.3
  227.1 0.0 all-reduce.2.cloned.1.call-start
  227.8 1.1 fusion.35
  228.9 8.2 %all-to-all-done = bf16[64,16,128]{2,0,1:T(8,128)(2,1)S(1)} async-done(((bf16[64,16,128]{2,0,1:T(8,128)(2,1)}), bf16[64,16,128]{2,0,1:T(8,128)(2,1)S(1)}, u32[]{:S(2)}, u32[]{:S(2)}) %all-to-all-start) | async-done | bytes 262176 | tf_op jit(solution)/shard_map/all_to_all | solution.py:72
  237.1 0.2 fusion.17
  237.4 0.0 copy-start.2
  237.4 0.2 fusion.64
  237.6 0.1 fusion.43
  237.7 0.1 pad_maximum_fusion.2
  237.8 0.1 multiply_convert_fusion
  237.9 1.3 collective-permute-start.2
  239.2 1.3 collective-permute-start.3
  240.5 1.3 collective-permute-start.4
  241.8 1.3 collective-permute-start.5
  243.1 0.0 copy-done.3
  243.1 0.7 fusion.50
  246.4 0.0 collective-permute-done.2
  246.4 0.2 conditional.4
  246.4 0.2 fusion
  246.6 0.0 collective-permute-done.3
  246.6 0.2 conditional.5
  246.6 0.2 fusion.1
  246.8 0.3 collective-permute-done.4
  247.1 0.2 conditional.6
  247.1 0.2 fusion.2
  247.3 3.1 collective-permute-done.5
  250.4 0.2 conditional.7
  250.4 0.2 fusion.3
  250.6 0.7 pad_maximum_fusion.1
  251.3 0.0 all-reduce.2.cloned.1.call-update
  251.3 90.1 %all-reduce.2.cloned.1.call-done = f32[4,128,128]{2,1,0:T(8,128)} async-done(((f32[4,128,128]{2,1,0:T(8,128)}), f32[4,128,128]{2,1,0:T(8,128)}) %all-reduce.2.cloned.1.call-update) | async-done | bytes 262160 | tf_op jit(solution)/shard_map/psum | solution.py:92
  341.4 0.0 copy-done.2
  341.4 2.1 fusion.22
  (4 shorter events, 0.0 us)
Async XLA Ops:
  6.5 5.4 %copy-start = (bf16[255]{0:T(256)(128)(2,1)S(1)}, bf16[255]{0:T(256)(128)(2,1)}, u32[]{:S(2)}) copy-start(bf16[255]{0:T(256)(128)(2,1)} %param.14) | copy-start | bytes 1534
  7.9 207.2 %collective-permute-start = (bf16[127,2048]{1,0:T(8,128)(2,1)S(1)}, bf16[127,2048]{1,0:T(8,128)(2,1)S(1)}, u32[]{:S(2)}, u32[]{:S(2)}) collective-permute-start(bf16[127,2048]{1,0:T(8,128)(2,1)S(1)} %get-tuple-element.49), channel_id=1, source_target_pairs={{0,1},{1,2},{2,3},{3,4},{4,5},{5,6},{6,7},{7,8},{8,9},{9,10},{10,1... | collective-permute-start | bytes 1560584 | tf_op jit(solution)/shard_map/ppermute | solution.py:16
  10.3 204.8 %collective-permute-start.1 = (bf16[127,2048]{1,0:T(8,128)(2,1)S(1)}, bf16[127,2048]{1,0:T(8,128)(2,1)}, u32[]{:S(2)}, u32[]{:S(2)}) collective-permute-start(bf16[127,2048]{1,0:T(8,128)(2,1)S(1)} %get-tuple-element.50), channel_id=1, source_target_pairs={{1,0},{2,1},{3,2},{4,3},{5,4},{6,5},{7,6},{8,7},{9,8},{10,9},{11,1... | collective-permute-start | bytes 1560584 | tf_op jit(solution)/shard_map/ppermute | solution.py:17
  12.0 203.2 %copy-start.1 = (bf16[320,2048]{1,0:T(8,128)(2,1)S(1)}, bf16[320,2048]{1,0:T(8,128)(2,1)}, u32[]{:S(2)}) copy-start(bf16[320,2048]{1,0:T(8,128)(2,1)} %param.13) | copy-start | bytes 3932164
  217.8 19.3 %all-to-all-start = ((bf16[64,16,128]{2,0,1:T(8,128)(2,1)}), bf16[64,16,128]{2,0,1:T(8,128)(2,1)S(1)}, u32[]{:S(2)}, u32[]{:S(2)}) async-start(bf16[64,16,128]{2,0,1:T(8,128)(2,1)} %bitcast.58), calls=%async_computation | async-start | bytes 524288 | tf_op jit(solution)/shard_map/all_to_all | solution.py:72
  227.1 16.0 %copy-start.3 = (s32[1,4]{1,0:T(1,128)S(1)}, s32[1,4]{1,0:T(1,128)}, u32[]{:S(2)}) copy-start(s32[1,4]{1,0:T(1,128)} %param.15) | copy-start | bytes 52
  227.1 114.3 %all-reduce.2.cloned.1.call-start = ((), (), s32[]{:S(2)}) async-start(), calls=%async_computation.1 | async-start | bytes 524288 | tf_op jit(solution)/shard_map/psum | solution.py:92
  237.4 104.1 %copy-start.2 = (s32[4]{0:T(128)S(1)}, s32[4]{0:T(128)}, u32[]{:S(2)}) copy-start(s32[4]{0:T(128)} %param.17) | copy-start | bytes 52
  237.9 8.5 %collective-permute-start.2 = (bf16[128,128]{1,0:T(8,128)(2,1)S(1)}, bf16[128,128]{1,0:T(8,128)(2,1)S(1)}, u32[]{:S(2)}, u32[]{:S(2)}) collective-permute-start(bf16[128,128]{1,0:T(8,128)(2,1)S(1)} %multiply_convert_fusion), channel_id=1, source_target_pairs={{1,0},{2,1},{3,2},{4,3},{5,4},{6,5},{7,6},{8,7},{9,8},{10,9},{11,1... | collective-permute-start | bytes 98312 | tf_op jit(solution)/shard_map/ppermute | solution.py:25
  239.2 7.4 %collective-permute-start.3 = (bf16[128,128]{1,0:T(8,128)(2,1)S(1)}, bf16[128,128]{1,0:T(8,128)(2,1)S(1)}, u32[]{:S(2)}, u32[]{:S(2)}) collective-permute-start(bf16[128,128]{1,0:T(8,128)(2,1)S(1)} %multiply_convert_fusion), channel_id=1, source_target_pairs={{2,0},{3,1},{4,2},{5,3},{6,4},{7,5},{8,6},{9,7},{10,8},{11,9},{12,... | collective-permute-start | bytes 98312 | tf_op jit(solution)/shard_map/ppermute | solution.py:25
  240.5 6.6 %collective-permute-start.4 = (bf16[128,128]{1,0:T(8,128)(2,1)S(1)}, bf16[128,128]{1,0:T(8,128)(2,1)S(1)}, u32[]{:S(2)}, u32[]{:S(2)}) collective-permute-start(bf16[128,128]{1,0:T(8,128)(2,1)S(1)} %multiply_convert_fusion), channel_id=1, source_target_pairs={{3,0},{4,1},{5,2},{6,3},{7,4},{8,5},{9,6},{10,7},{11,8},{12,9},{13... | collective-permute-start | bytes 98312 | tf_op jit(solution)/shard_map/ppermute | solution.py:25
  241.8 8.6 %collective-permute-start.5 = (bf16[128,128]{1,0:T(8,128)(2,1)S(1)}, bf16[128,128]{1,0:T(8,128)(2,1)S(1)}, u32[]{:S(2)}, u32[]{:S(2)}) collective-permute-start(bf16[128,128]{1,0:T(8,128)(2,1)S(1)} %multiply_convert_fusion), channel_id=1, source_target_pairs={{4,0},{5,1},{6,2},{7,3},{8,4},{9,5},{10,6},{11,7},{12,8},{13,9},{1... | collective-permute-start | bytes 98312 | tf_op jit(solution)/shard_map/ppermute | solution.py:25
Sparse Core Ops, SparseCore 0:
  251.5 89.9 all-reduce.1
where the time goes:
time: 351 us; the launch traced here: 350 us
  local copies, waits for them, and re-layouts  205 us (58%)
  waiting for transfers between devices  102 us (29%)
  starting transfers between devices  18.2 us (5%)
  between operations  16.8 us (5%)
  matrix products  5.15 us (1%)
    gather x2, local copies, waits for them, and re-layouts, band_matrix(): picked = jnp.take(taps, jnp.clip(offset, 0, width - 1))  203 us
    psum x1, waiting for transfers between devices, shards(): totals = lax.psum(stacked, 'chan')  90.1 us
    all_to_all x1, starting transfers between devices, shards(): lax.all_to_all(decimated, 'chan', split_axis=1, concat_axis=0, tiled=True)  9.27 us
    all_to_all x1, waiting for transfers between devices, shards(): lax.all_to_all(decimated, 'chan', split_axis=1, concat_axis=0, tiled=True)  8.22 us
  transfers between devices with their start and end apart: 8, of which 4 were waited for; matrix products, arithmetic and copies ran while one was open for 59% of the time, Pallas kernels for 0%

commit v1 on v0

--- a/solution.py
+++ b/solution.py
@@ -1,9 +1,14 @@
+import functools
 import math
 
 import jax
 import jax.numpy as jnp
 from jax import lax
+from jax.experimental import pallas as pl
+from jax.experimental.pallas import tpu as pltpu
 from jax.sharding import PartitionSpec as P
+
+MESH = pl.DeviceIdType.MESH
 
 
 def extended(x, sides, width):
@@ -26,14 +31,9 @@
 
 
 def band_matrix(taps, out_rows, in_cols):
-    width = taps.shape[0]
-    offset = (
-        jnp.arange(in_cols, dtype=jnp.int32)[None, :]
-        - 5 * jnp.arange(out_rows, dtype=jnp.int32)[:, None]
-    )
-    inside = (offset >= 0) & (offset < width)
-    picked = jnp.take(taps, jnp.clip(offset, 0, width - 1))
-    return jnp.where(inside, picked, jnp.zeros_like(picked))
+    period = in_cols + 5
+    padded = jnp.pad(taps, (0, period - taps.shape[0]))
+    return jnp.tile(padded, out_rows)[: out_rows * in_cols].reshape(out_rows, in_cols)
 
 
 def whiten(block):
@@ -60,7 +60,7 @@
     return product * scale
 
 
-def shards(raw, taps, tile_dist, tile_count, owner):
+def streamed(raw, taps, tile_dist, tile_count, owner):
     rows = raw.shape[0]
     width = taps.shape[0]
     half = (width - 1) // 2
@@ -75,7 +75,6 @@
     scale = 1.0 / whitened.shape[0]
     bands = tile_dist.shape[1]
     slots = jnp.arange(bands, dtype=jnp.int32) < tile_count[0]
-    partner = whitened
     stacks = []
     for distance in range(1, bands + 1):
         partner = passed_along(whitened, "chan", -distance)
@@ -94,6 +93,217 @@
     return jnp.einsum("b,bxy->xy", selected, totals, precision=lax.Precision.HIGHEST)[None]
 
 
+def split(x):
+    high = x.astype(jnp.bfloat16)
+    low = (x - high.astype(jnp.float32)).astype(jnp.bfloat16)
+    return high, low
+
+
+def mm(a, b):
+    return jnp.dot(a, b, preferred_element_type=jnp.float32)
+
+
+def fused_kernel(
+    n, width, bands,
+    dist_ref, count_ref, owner_ref, raw_ref, taps_ref, out_ref,
+    send1, recv1, send2, recv2, send3, ss1, rs1, ss2, rs2, ss3, rs3,
+):
+    me = lax.axis_index("chan")
+    rows, channels = raw_ref.shape
+    block = channels // n
+    steps = rows // 5
+    length = steps * n
+    bins = length // 16
+    mine = 2 * bins // n
+    hc = channels // 2
+    window = 128
+    lead = (window - steps) // 2
+
+    barrier = pltpu.get_barrier_semaphore()
+    for k in range(1, n):
+        pl.semaphore_signal(
+            barrier, inc=1, device_id={"chan": lax.rem(me + k, n)}, device_id_type=MESH
+        )
+
+    lanes = taps_ref.shape[1]
+    first = pltpu.roll(taps_ref[...], 0, 1, stride=5, stride_axis=0)
+    banded = jnp.concatenate(
+        [pltpu.roll(first, 40 * q, 1)[:, :384] for q in range(window // 8)], axis=0
+    ).astype(jnp.bfloat16)[:, :rows]
+    row = lax.broadcasted_iota(jnp.int32, (2 * bins, window), 0)
+    col = lax.broadcasted_iota(jnp.int32, (2 * bins, window), 1)
+    place = row % mine
+    freq = (row // mine) * (mine // 2) + place % (mine // 2) + 1
+    time = me * steps - lead + col
+    turn = (freq * time + jnp.where(place >= mine // 2, length // 4, 0)) & (length - 1)
+    table = jnp.cos(turn.astype(jnp.float32) * (2.0 * math.pi / length))
+    table = jnp.where((time >= 0) & (time < length), table, 0.0)
+    table_high, table_low = split(table)
+    gmap = mm(table_high, banded) + mm(table_low, banded)
+    gmap_high, gmap_low = split(gmap)
+
+    chunk = 256
+    for c in range(hc // chunk):
+        halves = []
+        for h in range(2):
+            part = raw_ref[:, h * hc + c * chunk : h * hc + (c + 1) * chunk]
+            spectra = mm(gmap_high, part) + mm(gmap_low, part)
+            halves.append(spectra.reshape(n, mine, chunk))
+        send1[:, :, c * chunk : (c + 1) * chunk] = jnp.concatenate(halves, axis=1).astype(
+            jnp.bfloat16
+        )
+    line = lax.broadcasted_iota(jnp.int32, (2 * mine, 128), 0)
+    info = jnp.zeros((2 * mine, 128), jnp.float32)
+    for d in range(bands):
+        listed = jnp.int32(0)
+        for s in range(bands):
+            hit = (dist_ref[0, s] == d + 1) & (s < count_ref[0])
+            listed = listed + hit.astype(jnp.int32)
+        info = jnp.where(line == d, listed.astype(jnp.float32), info)
+    send1[:, :, hc:] = jnp.broadcast_to(info[None], (n, 2 * mine, 128)).astype(jnp.bfloat16)
+
+    pl.semaphore_wait(barrier, n - 1)
+
+    def copy1(k):
+        to = lax.rem(me + k, n)
+        return pltpu.make_async_remote_copy(
+            src_ref=send1.at[to], dst_ref=recv1.at[me], send_sem=ss1.at[k],
+            recv_sem=rs1.at[k], device_id={"chan": to}, device_id_type=MESH,
+        )
+
+    def copy2(k):
+        to = lax.rem(me + k, n)
+        return pltpu.make_async_remote_copy(
+            src_ref=send2.at[to], dst_ref=recv2.at[me], send_sem=ss2.at[k],
+            recv_sem=rs2.at[k], device_id={"chan": to}, device_id_type=MESH,
+        )
+
+    share = block // n
+
+    def copy3(k):
+        to = lax.rem(me + k, n)
+        return pltpu.make_async_remote_copy(
+            src_ref=send3.at[to], dst_ref=out_ref.at[0, pl.ds(me * share, share)],
+            send_sem=ss3.at[k], recv_sem=rs3.at[k], device_id={"chan": to}, device_id_type=MESH,
+        )
+
+    for k in range(1, n):
+        copy1(k).start()
+    recv1[me] = send1[me]
+    for k in range(1, n):
+        copy1(k).wait_recv()
+    total = recv1[0, :, :hc].astype(jnp.float32)
+    for i in range(1, n):
+        total = total + recv1[i, :, :hc].astype(jnp.float32)
+
+    white = []
+    for j in range(n):
+        h, at = divmod(j * block, hc)
+        part = total[h * mine : (h + 1) * mine, at : at + block]
+        squares = part * part
+        squares = squares + pltpu.roll(squares, mine // 2, 0)
+        power = jnp.sum(squares, axis=1, keepdims=True) / (2 * block)
+        white.append(part * lax.rsqrt(power + 1e-06))
+    left = jnp.concatenate(white, axis=0).astype(jnp.bfloat16)
+    weights = [recv1[i, :, hc:].astype(jnp.float32) for i in range(n)]
+    rights = []
+    for d in range(bands):
+        pieces = []
+        for i in range(n):
+            if i + d + 1 < n:
+                pieces.append(white[i + d + 1] * weights[i][d : d + 1, :])
+            else:
+                pieces.append(jnp.zeros((mine, block), jnp.float32))
+        rights.append(jnp.concatenate(pieces, axis=0).astype(jnp.bfloat16))
+    right = jnp.concatenate(rights, axis=1)
+    stacks = lax.dot_general(
+        left, right, (((0,), (0,)), ((), ())), preferred_element_type=jnp.float32
+    )
+    hb = bands // 2 * block
+    stacks = jnp.concatenate(
+        [stacks[:, :hb].reshape(n, share, hb), stacks[:, hb:].reshape(n, share, hb)], axis=1
+    )
+    send2[...] = stacks.astype(jnp.bfloat16)
+
+    for k in range(1, n):
+        copy2(k).start()
+    recv2[me] = send2[me]
+    for k in range(1, n):
+        copy2(k).wait_recv()
+    total = recv2[0].astype(jnp.float32)
+    for i in range(1, n):
+        total = total + recv2[i].astype(jnp.float32)
+    total = total * (1.0 / (2 * bins))
+
+    for to in range(n):
+        chosen = jnp.zeros((share, block), jnp.float32)
+        for d in range(bands):
+            h, at = divmod(d * block, hb)
+            owned = (owner_ref[d] == to).astype(jnp.float32)
+            chosen = chosen + total[h * share : (h + 1) * share, at : at + block] * owned
+        send3[to] = chosen
+    for k in range(1, n):
+        copy3(k).start()
+    out_ref[0, pl.ds(me * share, share)] = send3[me]
+    for k in range(1, n):
+        copy3(k).wait_recv()
+    for k in range(1, n):
+        copy1(k).wait_send()
+        copy2(k).wait_send()
+        copy3(k).wait_send()
+
+
+def fused(raw, taps, tile_dist, tile_count, owner):
+    n = lax.axis_size("chan")
+    rows, channels = raw.shape
+    width = taps.shape[0]
+    half = (width - 1) // 2
+    bands = tile_dist.shape[1]
+    block = channels // n
+    steps = rows // 5
+    mine = 2 * (steps * n // 16) // n
+    lead = (128 - steps) // 2
+    lanes = 1024
+    start = lanes - 5 * lead - half
+    line = jnp.pad(taps.astype(jnp.float32), (start, lanes - start - width))
+    line = jnp.broadcast_to(line[None], (8, lanes))
+    vmem, smem = pl.BlockSpec(memory_space=pltpu.VMEM), pl.BlockSpec(memory_space=pltpu.SMEM)
+    share = block // n
+    sems = [pltpu.SemaphoreType.DMA((n,)) for _ in range(6)]
+    return pl.pallas_call(
+        functools.partial(fused_kernel, n, width, bands),
+        out_shape=jax.ShapeDtypeStruct((1, block, block), jnp.float32),
+        in_specs=[smem, smem, smem, vmem, vmem],
+        out_specs=vmem,
+        scratch_shapes=[
+            pltpu.VMEM((n, 2 * mine, channels // 2 + 128), jnp.bfloat16),
+            pltpu.VMEM((n, 2 * mine, channels // 2 + 128), jnp.bfloat16),
+            pltpu.VMEM((n, 2 * share, bands // 2 * block), jnp.bfloat16),
+            pltpu.VMEM((n, 2 * share, bands // 2 * block), jnp.bfloat16),
+            pltpu.VMEM((n, share, block), jnp.float32),
+            *sems,
+        ],
+        compiler_params=pltpu.CompilerParams(
+            collective_id=0, has_side_effects=True, vmem_limit_bytes=40 * 2**20
+        ),
+    )(tile_dist, tile_count, owner, raw, line)
+
+
+def shards(raw, taps, tile_dist, tile_count, owner):
+    n = lax.axis_size("chan")
+    rows, channels = raw.shape
+    steps = rows // 5
+    fits = (
+        channels == 128 * n
+        and n == 16
+        and rows == 320
+        and taps.shape[0] == 255
+        and tile_dist.shape[1] == 4
+    )
+    path = fused if fits else streamed
+    return path(raw, taps, tile_dist, tile_count, owner)
+
+
 def solution(mesh):
     in_specs = (P("chan", "groups"), P(), P("chan", "groups"), P(("groups", "chan")), P("groups"))
     out_specs = P("chan", "groups", None)

time: 351 us -> 37.1 us (0.11)
  local copies, waits for them, and re-layouts: 205 us -> 3.26 us
  waiting for transfers between devices: 102 us -> 0 us
  Pallas kernels: 0 us -> 32.2 us
  starting transfers between devices: 18.2 us -> 0 us
  between operations: 16.8 us -> 0.66 us
  matrix products: 5.15 us -> 0 us
    gather x2 -> x0, local copies, waits for them, and re-layouts: 203 us -> none  [band_matrix(): picked = jnp.take(taps, jnp.clip(offset, 0, width - 1))]
    psum x1 -> x0, waiting for transfers between devices: 90.1 us -> none  [shards(): totals = lax.psum(stacked, 'chan')]
    pallas_call x0 -> x1, Pallas kernels: none -> 32.2 us  [fused(): pl.pallas_call(functools.partial(fused_kernel, n, width, bands), out_shap...]
    all_to_all x1 -> x0, starting transfers between devices: 9.27 us -> none  [shards(): lax.all_to_all(decimated, 'chan', split_axis=1, concat_axis=0, tiled=True)]
    ppermute x6 -> x0, starting transfers between devices: 8.85 us -> none  [the longest x4 5.17 us: passed_along(): return lax.ppermute(x, axis, pairs)]
    all_to_all x1 -> x0, waiting for transfers between devices: 8.22 us -> none  [shards(): lax.all_to_all(decimated, 'chan', split_axis=1, concat_axis=0, tiled=True)]
    dot_general x8 -> x0, matrix products: 5.15 us -> none  [the longest x1 2.09 us: shards(): jnp.einsum('b,bxy->xy', selected, totals, precision=lax.Precision.HIGHEST)]
  transfers between devices with their start and end apart: 8 -> 0, of which waited for: 4 -> 0; matrix products, arithmetic and copies ran while one was open for 59% -> 0% of each run, Pallas kernels for 0% -> 0%
where the time goes in v1:
time: 37.1 us; the launch traced here: 36.9 us
  Pallas kernels  32.2 us (87%)
  local copies, waits for them, and re-layouts  3.26 us (9%)
  other arithmetic  0.73 us (2%)
  between operations  0.66 us (2%)
    pallas_call x1, Pallas kernels, fused(): pl.pallas_call(functools.partial(fused_kernel, n, width, bands), out_shap...  32.2 us
    unnamed x7, local copies, waits for them, and re-layouts  3.26 us

profile of v1, /device:TPU:0, one launch (start us, length us, event | category | flops | bytes accessed | tf_op | source)
XLA Modules:
  0.0 36.9 jit_solution(16367366848574197250)
XLA Ops:
  0.7 0.7 %pad_convert_fusion = f32[1024]{0:T(1024)S(1)} fusion(bf16[255]{0:T(256)(128)(2,1)} %param.6), kind=kLoop, calls=%fused_computation | loop fusion | flops 1024 | bytes 4606 | tf_op jit(solution)/shard_map/jit(_pad)/pad | solution.py:268
  1.4 0.0 copy-start
  1.4 1.3 %copy-done = bf16[320,2048]{1,0:T(8,128)(2,1)S(1)} copy-done((bf16[320,2048]{1,0:T(8,128)(2,1)S(1)}, bf16[320,2048]{1,0:T(8,128)(2,1)}, u32[]{:S(2)}) %copy-start) | copy-done | bytes 1310744
  2.7 0.0 copy-start.1
  2.7 0.7 %copy-done.1 = s32[1,4]{1,0:T(1,128)S(1)} copy-done((s32[1,4]{1,0:T(1,128)S(1)}, s32[1,4]{1,0:T(1,128)}, u32[]{:S(2)}) %copy-start.1) | copy-done | bytes 40
  3.4 0.0 copy-start.2
  3.4 0.7 %copy-done.2 = s32[4]{0:T(128)S(1)} copy-done((s32[4]{0:T(128)S(1)}, s32[4]{0:T(128)}, u32[]{:S(2)}) %copy-start.2) | copy-done | bytes 40
  4.0 32.2 %shard_map.55 = f32[1,128,128]{2,1,0:T(8,128)S(1)} custom-call(s32[1,4]{1,0:T(1,128)S(1)} %copy-done.1, s32[1]{0:T(128)S(6)} %copy.7.count_ref, s32[4]{0:T(128)S(1)} %copy-done.2, bf16[320,2048]{1,0:T(8,128)(2,1)S(1)} %copy-done, f32[8,1024]{1,0:T(8,128)S(1)} %broadcast_in_dim.2.taps_ref), custom_call_target="tpu_custom_call" | custom-call | tf_op jit(solution)/shard_map/pallas_call | solution.py:273
  36.3 0.6 %copy.8 = f32[1,128,128]{2,1,0:T(8,128)} copy(f32[1,128,128]{2,1,0:T(8,128)S(1)} %shard_map.55) | data formatting | bytes 131072
  (1 shorter events, 0.0 us)
Async XLA Ops:
  1.4 1.3 %copy-start = (bf16[320,2048]{1,0:T(8,128)(2,1)S(1)}, bf16[320,2048]{1,0:T(8,128)(2,1)}, u32[]{:S(2)}) copy-start(bf16[320,2048]{1,0:T(8,128)(2,1)} %raw_ref.1) | copy-start | bytes 3932164
  2.7 0.7 %copy-start.1 = (s32[1,4]{1,0:T(1,128)S(1)}, s32[1,4]{1,0:T(1,128)}, u32[]{:S(2)}) copy-start(s32[1,4]{1,0:T(1,128)} %dist_ref.1) | copy-start | bytes 52
  3.4 0.7 %copy-start.2 = (s32[4]{0:T(128)S(1)}, s32[4]{0:T(128)}, u32[]{:S(2)}) copy-start(s32[4]{0:T(128)} %owner_ref.1) | copy-start | bytes 52

commit v2 on v1

--- a/solution.py
+++ b/solution.py
@@ -106,9 +106,11 @@
 def fused_kernel(
     n, width, bands,
     dist_ref, count_ref, owner_ref, raw_ref, taps_ref, out_ref,
-    send1, recv1, send2, recv2, send3, ss1, rs1, ss2, rs2, ss3, rs3,
+    both, pair, send1, recv1, send2, recv2, send3, ss0, rs0, ss1, rs1, ss2, rs2, ss3, rs3,
 ):
     me = lax.axis_index("chan")
+    chips = n // 2
+    chip, core = me // 2, me % 2
     rows, channels = raw_ref.shape
     block = channels // n
     steps = rows // 5
@@ -133,7 +135,9 @@
     row = lax.broadcasted_iota(jnp.int32, (2 * bins, window), 0)
     col = lax.broadcasted_iota(jnp.int32, (2 * bins, window), 1)
     place = row % mine
-    freq = (row // mine) * (mine // 2) + place % (mine // 2) + 1
+    order = row // mine
+    holder = (order % chips) * 2 + order // chips
+    freq = holder * (mine // 2) + place % (mine // 2) + 1
     time = me * steps - lead + col
     turn = (freq * time + jnp.where(place >= mine // 2, length // 4, 0)) & (length - 1)
     table = jnp.cos(turn.astype(jnp.float32) * (2.0 * math.pi / length))
@@ -149,7 +153,7 @@
             part = raw_ref[:, h * hc + c * chunk : h * hc + (c + 1) * chunk]
             spectra = mm(gmap_high, part) + mm(gmap_low, part)
             halves.append(spectra.reshape(n, mine, chunk))
-        send1[:, :, c * chunk : (c + 1) * chunk] = jnp.concatenate(halves, axis=1).astype(
+        both[:, :, c * chunk : (c + 1) * chunk] = jnp.concatenate(halves, axis=1).astype(
             jnp.bfloat16
         )
     line = lax.broadcasted_iota(jnp.int32, (2 * mine, 128), 0)
@@ -159,16 +163,21 @@
         for s in range(bands):
             hit = (dist_ref[0, s] == d + 1) & (s < count_ref[0])
             listed = listed + hit.astype(jnp.int32)
-        info = jnp.where(line == d, listed.astype(jnp.float32), info)
-    send1[:, :, hc:] = jnp.broadcast_to(info[None], (n, 2 * mine, 128)).astype(jnp.bfloat16)
+        info = jnp.where(line == core * mine + d, listed.astype(jnp.float32), info)
+    both[:, :, hc:] = jnp.broadcast_to(info[None], (n, 2 * mine, 128)).astype(jnp.bfloat16)
 
     pl.semaphore_wait(barrier, n - 1)
 
+    first_copy = pltpu.make_async_remote_copy(
+        src_ref=both.at[pl.ds((1 - core) * chips, chips)], dst_ref=pair, send_sem=ss0,
+        recv_sem=rs0, device_id={"chan": chip * 2 + 1 - core}, device_id_type=MESH,
+    )
+
     def copy1(k):
-        to = lax.rem(me + k, n)
+        to = lax.rem(chip + k, chips)
         return pltpu.make_async_remote_copy(
-            src_ref=send1.at[to], dst_ref=recv1.at[me], send_sem=ss1.at[k],
-            recv_sem=rs1.at[k], device_id={"chan": to}, device_id_type=MESH,
+            src_ref=send1.at[to], dst_ref=recv1.at[chip], send_sem=ss1.at[k],
+            recv_sem=rs1.at[k], device_id={"chan": to * 2 + core}, device_id_type=MESH,
         )
 
     def copy2(k):
@@ -187,13 +196,19 @@
             send_sem=ss3.at[k], recv_sem=rs3.at[k], device_id={"chan": to}, device_id_type=MESH,
         )
 
-    for k in range(1, n):
+    first_copy.start()
+    first_copy.wait_recv()
+    for k in range(1, chips):
+        to = lax.rem(chip + k, chips)
+        own = both[core * chips + to].astype(jnp.float32)
+        send1[to] = (own + pair[to].astype(jnp.float32)).astype(jnp.bfloat16)
         copy1(k).start()
-    recv1[me] = send1[me]
-    for k in range(1, n):
+    own = both[core * chips + chip].astype(jnp.float32)
+    recv1[chip] = (own + pair[chip].astype(jnp.float32)).astype(jnp.bfloat16)
+    for k in range(1, chips):
         copy1(k).wait_recv()
     total = recv1[0, :, :hc].astype(jnp.float32)
-    for i in range(1, n):
+    for i in range(1, chips):
         total = total + recv1[i, :, :hc].astype(jnp.float32)
 
     white = []
@@ -205,13 +220,13 @@
         power = jnp.sum(squares, axis=1, keepdims=True) / (2 * block)
         white.append(part * lax.rsqrt(power + 1e-06))
     left = jnp.concatenate(white, axis=0).astype(jnp.bfloat16)
-    weights = [recv1[i, :, hc:].astype(jnp.float32) for i in range(n)]
+    weights = [recv1[i, :, hc:].astype(jnp.float32) for i in range(chips)]
     rights = []
     for d in range(bands):
         pieces = []
         for i in range(n):
             if i + d + 1 < n:
-                pieces.append(white[i + d + 1] * weights[i][d : d + 1, :])
+                pieces.append(white[i + d + 1] * weights[i // 2][i % 2 * mine + d : i % 2 * mine + d + 1, :])
             else:
                 pieces.append(jnp.zeros((mine, block), jnp.float32))
         rights.append(jnp.concatenate(pieces, axis=0).astype(jnp.bfloat16))
@@ -247,8 +262,10 @@
     out_ref[0, pl.ds(me * share, share)] = send3[me]
     for k in range(1, n):
         copy3(k).wait_recv()
-    for k in range(1, n):
+    first_copy.wait_send()
+    for k in range(1, chips):
         copy1(k).wait_send()
+    for k in range(1, n):
         copy2(k).wait_send()
         copy3(k).wait_send()
 
@@ -277,10 +294,14 @@
         out_specs=vmem,
         scratch_shapes=[
             pltpu.VMEM((n, 2 * mine, channels // 2 + 128), jnp.bfloat16),
-            pltpu.VMEM((n, 2 * mine, channels // 2 + 128), jnp.bfloat16),
+            pltpu.VMEM((n // 2, 2 * mine, channels // 2 + 128), jnp.bfloat16),
+            pltpu.VMEM((n // 2, 2 * mine, channels // 2 + 128), jnp.bfloat16),
+            pltpu.VMEM((n // 2, 2 * mine, channels // 2 + 128), jnp.bfloat16),
             pltpu.VMEM((n, 2 * share, bands // 2 * block), jnp.bfloat16),
             pltpu.VMEM((n, 2 * share, bands // 2 * block), jnp.bfloat16),
             pltpu.VMEM((n, share, block), jnp.float32),
+            pltpu.SemaphoreType.DMA,
+            pltpu.SemaphoreType.DMA,
             *sems,
         ],
         compiler_params=pltpu.CompilerParams(

time: 37.1 us -> 30.9 us (0.83)
  Pallas kernels: 32.2 us -> 26.1 us
    pallas_call x1, Pallas kernels: 32.2 us -> 26.1 us  [fused(): pl.pallas_call(functools.partial(fused_kernel, n, width, bands), out_shap...]
where the time goes in v2:
time: 30.9 us; the launch traced here: 30.8 us
  Pallas kernels  26.1 us (84%)
  local copies, waits for them, and re-layouts  3.26 us (11%)
  other arithmetic  0.73 us (2%)
  between operations  0.66 us (2%)
    pallas_call x1, Pallas kernels, fused(): pl.pallas_call(functools.partial(fused_kernel, n, width, bands), out_shap...  26.1 us
    unnamed x7, local copies, waits for them, and re-layouts  3.26 us
    pad x1, other arithmetic, fused(): line = jnp.pad(taps.astype(jnp.float32), (start, lanes - start - width))  0.73 us

profile of v2, /device:TPU:0, one launch (start us, length us, event | category | flops | bytes accessed | tf_op | source)
XLA Modules:
  0.0 30.8 jit_solution(15569601258929575715)
XLA Ops:
  0.7 0.7 %pad_convert_fusion = f32[1024]{0:T(1024)S(1)} fusion(bf16[255]{0:T(256)(128)(2,1)} %param.6), kind=kLoop, calls=%fused_computation | loop fusion | flops 1024 | bytes 4606 | tf_op jit(solution)/shard_map/jit(_pad)/pad | solution.py:285
  1.4 0.0 copy-start
  1.4 1.3 %copy-done = bf16[320,2048]{1,0:T(8,128)(2,1)S(1)} copy-done((bf16[320,2048]{1,0:T(8,128)(2,1)S(1)}, bf16[320,2048]{1,0:T(8,128)(2,1)}, u32[]{:S(2)}) %copy-start) | copy-done | bytes 1310744
  2.7 0.0 copy-start.1
  2.7 0.7 %copy-done.1 = s32[1,4]{1,0:T(1,128)S(1)} copy-done((s32[1,4]{1,0:T(1,128)S(1)}, s32[1,4]{1,0:T(1,128)}, u32[]{:S(2)}) %copy-start.1) | copy-done | bytes 40
  3.4 0.0 copy-start.2
  3.4 0.7 %copy-done.2 = s32[4]{0:T(128)S(1)} copy-done((s32[4]{0:T(128)S(1)}, s32[4]{0:T(128)}, u32[]{:S(2)}) %copy-start.2) | copy-done | bytes 40
  4.0 26.1 %shard_map.55 = f32[1,128,128]{2,1,0:T(8,128)S(1)} custom-call(s32[1,4]{1,0:T(1,128)S(1)} %copy-done.1, s32[1]{0:T(128)S(6)} %copy.7.count_ref, s32[4]{0:T(128)S(1)} %copy-done.2, bf16[320,2048]{1,0:T(8,128)(2,1)S(1)} %copy-done, f32[8,1024]{1,0:T(8,128)S(1)} %broadcast_in_dim.2.taps_ref), custom_call_target="tpu_custom_call" | custom-call | tf_op jit(solution)/shard_map/pallas_call | solution.py:290
  30.1 0.6 %copy.8 = f32[1,128,128]{2,1,0:T(8,128)} copy(f32[1,128,128]{2,1,0:T(8,128)S(1)} %shard_map.55) | data formatting | bytes 131072
  (1 shorter events, 0.0 us)
Async XLA Ops:
  1.4 1.3 %copy-start = (bf16[320,2048]{1,0:T(8,128)(2,1)S(1)}, bf16[320,2048]{1,0:T(8,128)(2,1)}, u32[]{:S(2)}) copy-start(bf16[320,2048]{1,0:T(8,128)(2,1)} %raw_ref.1) | copy-start | bytes 3932164
  2.7 0.7 %copy-start.1 = (s32[1,4]{1,0:T(1,128)S(1)}, s32[1,4]{1,0:T(1,128)}, u32[]{:S(2)}) copy-start(s32[1,4]{1,0:T(1,128)} %dist_ref.1) | copy-start | bytes 52
  3.4 0.7 %copy-start.2 = (s32[4]{0:T(128)S(1)}, s32[4]{0:T(128)}, u32[]{:S(2)}) copy-start(s32[4]{0:T(128)} %owner_ref.1) | copy-start | bytes 52

commit v3 on v2

--- a/solution.py
+++ b/solution.py
@@ -105,8 +105,8 @@
 
 def fused_kernel(
     n, width, bands,
-    dist_ref, count_ref, owner_ref, raw_ref, taps_ref, out_ref,
-    both, pair, send1, recv1, send2, recv2, send3, ss0, rs0, ss1, rs1, ss2, rs2, ss3, rs3,
+    dist_hbm, count_hbm, owner_hbm, raw_hbm, taps_ref, out_ref,
+    dist_ref, count_ref, owner_ref, raw_ref, loads, both, pair, send1, recv1, both2, pair2, send2, recv2, send3, ss0, rs0, ss4, rs4, ss1, rs1, ss2, rs2, ss3, rs3,
 ):
     me = lax.axis_index("chan")
     chips = n // 2
@@ -121,6 +121,19 @@
     window = 128
     lead = (window - steps) // 2
 
+    loaded = [
+        pltpu.make_async_copy(source, held, loads.at[at])
+        for at, (source, held) in enumerate(
+            [
+                (raw_hbm, raw_ref),
+                (dist_hbm, dist_ref),
+                (count_hbm, count_ref),
+                (owner_hbm, owner_ref),
+            ]
+        )
+    ]
+    for load in loaded:
+        load.start()
     barrier = pltpu.get_barrier_semaphore()
     for k in range(1, n):
         pl.semaphore_signal(
@@ -146,6 +159,8 @@
     gmap = mm(table_high, banded) + mm(table_low, banded)
     gmap_high, gmap_low = split(gmap)
 
+    for load in loaded:
+        load.wait()
     chunk = 256
     for c in range(hc // chunk):
         halves = []
@@ -180,19 +195,25 @@
             recv_sem=rs1.at[k], device_id={"chan": to * 2 + core}, device_id_type=MESH,
         )
 
+    second_copy = pltpu.make_async_remote_copy(
+        src_ref=both2.at[pl.ds((1 - core) * chips, chips)], dst_ref=pair2, send_sem=ss4,
+        recv_sem=rs4, device_id={"chan": chip * 2 + 1 - core}, device_id_type=MESH,
+    )
+
     def copy2(k):
-        to = lax.rem(me + k, n)
+        to = lax.rem(chip + k, chips)
         return pltpu.make_async_remote_copy(
-            src_ref=send2.at[to], dst_ref=recv2.at[me], send_sem=ss2.at[k],
-            recv_sem=rs2.at[k], device_id={"chan": to}, device_id_type=MESH,
+            src_ref=send2.at[to], dst_ref=recv2.at[chip], send_sem=ss2.at[k],
+            recv_sem=rs2.at[k], device_id={"chan": to * 2 + core}, device_id_type=MESH,
         )
 
     share = block // n
+    place = (core * chips + chip) * share
 
     def copy3(k):
         to = lax.rem(me + k, n)
         return pltpu.make_async_remote_copy(
-            src_ref=send3.at[to], dst_ref=out_ref.at[0, pl.ds(me * share, share)],
+            src_ref=send3.at[to], dst_ref=out_ref.at[0, pl.ds(place, share)],
             send_sem=ss3.at[k], recv_sem=rs3.at[k], device_id={"chan": to}, device_id_type=MESH,
         )
 
@@ -238,15 +259,21 @@
     stacks = jnp.concatenate(
         [stacks[:, :hb].reshape(n, share, hb), stacks[:, hb:].reshape(n, share, hb)], axis=1
     )
-    send2[...] = stacks.astype(jnp.bfloat16)
-
-    for k in range(1, n):
+    both2[...] = stacks.astype(jnp.bfloat16)
+
+    second_copy.start()
+    second_copy.wait_recv()
+    for k in range(1, chips):
+        to = lax.rem(chip + k, chips)
+        own = both2[core * chips + to].astype(jnp.float32)
+        send2[to] = (own + pair2[to].astype(jnp.float32)).astype(jnp.bfloat16)
         copy2(k).start()
-    recv2[me] = send2[me]
-    for k in range(1, n):
+    own = both2[core * chips + chip].astype(jnp.float32)
+    recv2[chip] = (own + pair2[chip].astype(jnp.float32)).astype(jnp.bfloat16)
+    for k in range(1, chips):
         copy2(k).wait_recv()
     total = recv2[0].astype(jnp.float32)
-    for i in range(1, n):
+    for i in range(1, chips):
         total = total + recv2[i].astype(jnp.float32)
     total = total * (1.0 / (2 * bins))
 
@@ -259,14 +286,16 @@
         send3[to] = chosen
     for k in range(1, n):
         copy3(k).start()
-    out_ref[0, pl.ds(me * share, share)] = send3[me]
+    out_ref[0, pl.ds(place, share)] = send3[me]
     for k in range(1, n):
         copy3(k).wait_recv()
     first_copy.wait_send()
     for k in range(1, chips):
         copy1(k).wait_send()
+    second_copy.wait_send()
+    for k in range(1, chips):
+        copy2(k).wait_send()
     for k in range(1, n):
-        copy2(k).wait_send()
         copy3(k).wait_send()
 
 
@@ -284,28 +313,34 @@
     start = lanes - 5 * lead - half
     line = jnp.pad(taps.astype(jnp.float32), (start, lanes - start - width))
     line = jnp.broadcast_to(line[None], (8, lanes))
-    vmem, smem = pl.BlockSpec(memory_space=pltpu.VMEM), pl.BlockSpec(memory_space=pltpu.SMEM)
+    vmem, hbm = pl.BlockSpec(memory_space=pltpu.VMEM), pl.BlockSpec(memory_space=pltpu.HBM)
     share = block // n
     sems = [pltpu.SemaphoreType.DMA((n,)) for _ in range(6)]
     return pl.pallas_call(
         functools.partial(fused_kernel, n, width, bands),
         out_shape=jax.ShapeDtypeStruct((1, block, block), jnp.float32),
-        in_specs=[smem, smem, smem, vmem, vmem],
+        in_specs=[hbm, hbm, hbm, hbm, vmem],
         out_specs=vmem,
         scratch_shapes=[
+            pltpu.SMEM(tile_dist.shape, jnp.int32),
+            pltpu.SMEM(tile_count.shape, jnp.int32),
+            pltpu.SMEM(owner.shape, jnp.int32),
+            pltpu.VMEM(raw.shape, raw.dtype),
+            pltpu.SemaphoreType.DMA((4,)),
             pltpu.VMEM((n, 2 * mine, channels // 2 + 128), jnp.bfloat16),
             pltpu.VMEM((n // 2, 2 * mine, channels // 2 + 128), jnp.bfloat16),
             pltpu.VMEM((n // 2, 2 * mine, channels // 2 + 128), jnp.bfloat16),
             pltpu.VMEM((n // 2, 2 * mine, channels // 2 + 128), jnp.bfloat16),
             pltpu.VMEM((n, 2 * share, bands // 2 * block), jnp.bfloat16),
-            pltpu.VMEM((n, 2 * share, bands // 2 * block), jnp.bfloat16),
+            pltpu.VMEM((n // 2, 2 * share, bands // 2 * block), jnp.bfloat16),
+            pltpu.VMEM((n // 2, 2 * share, bands // 2 * block), jnp.bfloat16),
+            pltpu.VMEM((n // 2, 2 * share, bands // 2 * block), jnp.bfloat16),
             pltpu.VMEM((n, share, block), jnp.float32),
-            pltpu.SemaphoreType.DMA,
-            pltpu.SemaphoreType.DMA,
+            *[pltpu.SemaphoreType.DMA] * 4,
             *sems,
         ],
         compiler_params=pltpu.CompilerParams(
-            collective_id=0, has_side_effects=True, vmem_limit_bytes=40 * 2**20
+            collective_id=0, has_side_effects=True, vmem_limit_bytes=61 * 2**20
         ),
     )(tile_dist, tile_count, owner, raw, line)
 

time: 30.9 us -> 30.5 us (0.987)
  local copies, waits for them, and re-layouts: 3.26 us -> 2.09 us
  Pallas kernels: 26.1 us -> 26.8 us
    unnamed x7 -> x1, local copies, waits for them, and re-layouts: 3.26 us -> 1.47 us
    pallas_call x1, Pallas kernels: 26.1 us -> 26.8 us  [fused(): pl.pallas_call(functools.partial(fused_kernel, n, width, bands), out_shap...]
    broadcast_in_dim x1, local copies, waits for them, and re-layouts: 0.01 us -> 0.62 us  [fused(): line = jnp.broadcast_to(line[None], (8, lanes))]
where the time goes in v3:
time: 30.5 us; the launch traced here: 30.2 us
  Pallas kernels  26.8 us (88%)
  local copies, waits for them, and re-layouts  2.09 us (7%)
  other arithmetic  0.73 us (2%)
  between operations  0.66 us (2%)
    pallas_call x1, Pallas kernels, fused(): pl.pallas_call(functools.partial(fused_kernel, n, width, bands), out_shap...  26.8 us
    unnamed x1, local copies, waits for them, and re-layouts  1.47 us
    pad x1, other arithmetic, fused(): line = jnp.pad(taps.astype(jnp.float32), (start, lanes - start - width))  0.73 us
    broadcast_in_dim x1, local copies, waits for them, and re-layouts, fused(): line = jnp.broadcast_to(line[None], (8, lanes))  0.62 us

profile of v3, /device:TPU:0, one launch (start us, length us, event | category | flops | bytes accessed | tf_op | source)
XLA Modules:
  0.0 30.2 jit_solution(8219080129410049681)
XLA Ops:
  0.7 0.7 %pad_convert_fusion = f32[1024]{0:T(1024)S(1)} fusion(bf16[255]{0:T(256)(128)(2,1)} %param.6), kind=kLoop, calls=%fused_computation | loop fusion | flops 1024 | bytes 4606 | tf_op jit(solution)/shard_map/jit(_pad)/pad | solution.py:314
  1.4 0.6 %broadcast_in_dim.2.taps_ref = f32[8,1024]{1,0:T(8,128)} broadcast(f32[1024]{0:T(1024)S(1)} %pad_convert_fusion), dimensions={1} | broadcast | bytes 36864 | tf_op jit(solution)/shard_map/broadcast_in_dim | solution.py:315
  2.0 26.8 %shard_map.55 = f32[1,128,128]{2,1,0:T(8,128)} custom-call(s32[1,4]{1,0:T(1,128)} %dist_hbm.1, s32[1]{0:T(128)S(6)} %copy.7.count_hbm, s32[4]{0:T(128)} %owner_hbm.1, bf16[320,2048]{1,0:T(8,128)(2,1)} %raw_hbm.1, f32[8,1024]{1,0:T(8,128)} %broadcast_in_dim.2.taps_ref), custom_call_target="tpu_custom_call" | custom-call | tf_op jit(solution)/shard_map/pallas_call | solution.py:319
  28.8 1.5 %copy.8 = f32[1,128,128]{2,1,0:T(8,128)} copy(f32[1,128,128]{2,1,0:T(8,128)} %shard_map.55) | data formatting | bytes 131072

commit v4 on v3

--- a/solution.py
+++ b/solution.py
@@ -162,7 +162,8 @@
     for load in loaded:
         load.wait()
     chunk = 256
-    for c in range(hc // chunk):
+
+    def transform(c):
         halves = []
         for h in range(2):
             part = raw_ref[:, h * hc + c * chunk : h * hc + (c + 1) * chunk]
@@ -171,6 +172,10 @@
         both[:, :, c * chunk : (c + 1) * chunk] = jnp.concatenate(halves, axis=1).astype(
             jnp.bfloat16
         )
+
+    pieces = [(0, hc // 2), (hc // 2, hc // 2 + 128)]
+    for c in range(hc // chunk // 2):
+        transform(c)
     line = lax.broadcasted_iota(jnp.int32, (2 * mine, 128), 0)
     info = jnp.zeros((2 * mine, 128), jnp.float32)
     for d in range(bands):
@@ -183,16 +188,21 @@
 
     pl.semaphore_wait(barrier, n - 1)
 
-    first_copy = pltpu.make_async_remote_copy(
-        src_ref=both.at[pl.ds((1 - core) * chips, chips)], dst_ref=pair, send_sem=ss0,
-        recv_sem=rs0, device_id={"chan": chip * 2 + 1 - core}, device_id_type=MESH,
-    )
-
-    def copy1(k):
+    def copy0(p):
+        cols = pl.ds(*pieces[p])
+        return pltpu.make_async_remote_copy(
+            src_ref=both.at[pl.ds((1 - core) * chips, chips), :, cols],
+            dst_ref=pair.at[:, :, cols], send_sem=ss0.at[p], recv_sem=rs0.at[p],
+            device_id={"chan": chip * 2 + 1 - core}, device_id_type=MESH,
+        )
+
+    def copy1(p, k):
         to = lax.rem(chip + k, chips)
+        cols = pl.ds(*pieces[p])
         return pltpu.make_async_remote_copy(
-            src_ref=send1.at[to], dst_ref=recv1.at[chip], send_sem=ss1.at[k],
-            recv_sem=rs1.at[k], device_id={"chan": to * 2 + core}, device_id_type=MESH,
+            src_ref=send1.at[to, :, cols], dst_ref=recv1.at[chip, :, cols],
+            send_sem=ss1.at[p * chips + k], recv_sem=rs1.at[p * chips + k],
+            device_id={"chan": to * 2 + core}, device_id_type=MESH,
         )
 
     second_copy = pltpu.make_async_remote_copy(
@@ -217,17 +227,23 @@
             send_sem=ss3.at[k], recv_sem=rs3.at[k], device_id={"chan": to}, device_id_type=MESH,
         )
 
-    first_copy.start()
-    first_copy.wait_recv()
-    for k in range(1, chips):
-        to = lax.rem(chip + k, chips)
-        own = both[core * chips + to].astype(jnp.float32)
-        send1[to] = (own + pair[to].astype(jnp.float32)).astype(jnp.bfloat16)
-        copy1(k).start()
-    own = both[core * chips + chip].astype(jnp.float32)
-    recv1[chip] = (own + pair[chip].astype(jnp.float32)).astype(jnp.bfloat16)
-    for k in range(1, chips):
-        copy1(k).wait_recv()
+    copy0(0).start()
+    for c in range(hc // chunk // 2, hc // chunk):
+        transform(c)
+    copy0(1).start()
+    for p in range(2):
+        cols = slice(pieces[p][0], sum(pieces[p]))
+        copy0(p).wait_recv()
+        for k in range(1, chips):
+            to = lax.rem(chip + k, chips)
+            own = both[core * chips + to, :, cols].astype(jnp.float32)
+            send1[to, :, cols] = (own + pair[to, :, cols].astype(jnp.float32)).astype(jnp.bfloat16)
+            copy1(p, k).start()
+        own = both[core * chips + chip, :, cols].astype(jnp.float32)
+        recv1[chip, :, cols] = (own + pair[chip, :, cols].astype(jnp.float32)).astype(jnp.bfloat16)
+    for p in range(2):
+        for k in range(1, chips):
+            copy1(p, k).wait_recv()
     total = recv1[0, :, :hc].astype(jnp.float32)
     for i in range(1, chips):
         total = total + recv1[i, :, :hc].astype(jnp.float32)
@@ -244,13 +260,13 @@
     weights = [recv1[i, :, hc:].astype(jnp.float32) for i in range(chips)]
     rights = []
     for d in range(bands):
-        pieces = []
+        tiles = []
         for i in range(n):
             if i + d + 1 < n:
-                pieces.append(white[i + d + 1] * weights[i // 2][i % 2 * mine + d : i % 2 * mine + d + 1, :])
+                tiles.append(white[i + d + 1] * weights[i // 2][i % 2 * mine + d : i % 2 * mine + d + 1, :])
             else:
-                pieces.append(jnp.zeros((mine, block), jnp.float32))
-        rights.append(jnp.concatenate(pieces, axis=0).astype(jnp.bfloat16))
+                tiles.append(jnp.zeros((mine, block), jnp.float32))
+        rights.append(jnp.concatenate(tiles, axis=0).astype(jnp.bfloat16))
     right = jnp.concatenate(rights, axis=1)
     stacks = lax.dot_general(
         left, right, (((0,), (0,)), ((), ())), preferred_element_type=jnp.float32
@@ -289,9 +305,10 @@
     out_ref[0, pl.ds(place, share)] = send3[me]
     for k in range(1, n):
         copy3(k).wait_recv()
-    first_copy.wait_send()
-    for k in range(1, chips):
-        copy1(k).wait_send()
+    for p in range(2):
+        copy0(p).wait_send()
+        for k in range(1, chips):
+            copy1(p, k).wait_send()
     second_copy.wait_send()
     for k in range(1, chips):
         copy2(k).wait_send()
@@ -336,7 +353,10 @@
             pltpu.VMEM((n // 2, 2 * share, bands // 2 * block), jnp.bfloat16),
             pltpu.VMEM((n // 2, 2 * share, bands // 2 * block), jnp.bfloat16),
             pltpu.VMEM((n, share, block), jnp.float32),
-            *[pltpu.SemaphoreType.DMA] * 4,
+            pltpu.SemaphoreType.DMA((2,)),
+            pltpu.SemaphoreType.DMA((2,)),
+            pltpu.SemaphoreType.DMA,
+            pltpu.SemaphoreType.DMA,
             *sems,
         ],
         compiler_params=pltpu.CompilerParams(

time: 30.5 us -> 30.4 us (level)
  no operation moved by 1% of the time
where the time goes in v4:
time: 30.4 us; the launch traced here: 30.1 us
  Pallas kernels  26.6 us (88%)
  local copies, waits for them, and re-layouts  2.09 us (7%)
  other arithmetic  0.73 us (2%)
  between operations  0.66 us (2%)
    pallas_call x1, Pallas kernels, fused(): pl.pallas_call(functools.partial(fused_kernel, n, width, bands), out_shap...  26.6 us
    unnamed x1, local copies, waits for them, and re-layouts  1.47 us
    pad x1, other arithmetic, fused(): line = jnp.pad(taps.astype(jnp.float32), (start, lanes - start - width))  0.73 us
    broadcast_in_dim x1, local copies, waits for them, and re-layouts, fused(): line = jnp.broadcast_to(line[None], (8, lanes))  0.62 us

profile of v4, /device:TPU:0, one launch (start us, length us, event | category | flops | bytes accessed | tf_op | source)
XLA Modules:
  0.0 30.1 jit_solution(14160986081496465091)
XLA Ops:
  0.7 0.7 %pad_convert_fusion = f32[1024]{0:T(1024)S(1)} fusion(bf16[255]{0:T(256)(128)(2,1)} %param.6), kind=kLoop, calls=%fused_computation | loop fusion | flops 1024 | bytes 4606 | tf_op jit(solution)/shard_map/jit(_pad)/pad | solution.py:331
  1.4 0.6 %broadcast_in_dim.2.taps_ref = f32[8,1024]{1,0:T(8,128)} broadcast(f32[1024]{0:T(1024)S(1)} %pad_convert_fusion), dimensions={1} | broadcast | bytes 36864 | tf_op jit(solution)/shard_map/broadcast_in_dim | solution.py:332
  2.0 26.6 %shard_map.55 = f32[1,128,128]{2,1,0:T(8,128)} custom-call(s32[1,4]{1,0:T(1,128)} %dist_hbm.1, s32[1]{0:T(128)S(6)} %copy.7.count_hbm, s32[4]{0:T(128)} %owner_hbm.1, bf16[320,2048]{1,0:T(8,128)(2,1)} %raw_hbm.1, f32[8,1024]{1,0:T(8,128)} %broadcast_in_dim.2.taps_ref), custom_call_target="tpu_custom_call" | custom-call | tf_op jit(solution)/shard_map/pallas_call | solution.py:336
  28.6 1.5 %copy.8 = f32[1,128,128]{2,1,0:T(8,128)} copy(f32[1,128,128]{2,1,0:T(8,128)} %shard_map.55) | data formatting | bytes 131072

commit v5 on v4

--- a/solution.py
+++ b/solution.py
@@ -105,8 +105,8 @@
 
 def fused_kernel(
     n, width, bands,
-    dist_hbm, count_hbm, owner_hbm, raw_hbm, taps_ref, out_ref,
-    dist_ref, count_ref, owner_ref, raw_ref, loads, both, pair, send1, recv1, both2, pair2, send2, recv2, send3, ss0, rs0, ss4, rs4, ss1, rs1, ss2, rs2, ss3, rs3,
+    plan_hbm, raw_hbm, taps_ref, out_ref,
+    plan_ref, raw_ref, loads, both, pair, send1, recv1, both2, pair2, send2, recv2, send3, ss0, rs0, ss4, rs4, ss1, rs1, ss2, rs2, ss3, rs3,
 ):
     me = lax.axis_index("chan")
     chips = n // 2
@@ -126,9 +126,7 @@
         for at, (source, held) in enumerate(
             [
                 (raw_hbm, raw_ref),
-                (dist_hbm, dist_ref),
-                (count_hbm, count_ref),
-                (owner_hbm, owner_ref),
+                (plan_hbm, plan_ref),
             ]
         )
     ]
@@ -141,7 +139,8 @@
         )
 
     lanes = taps_ref.shape[1]
-    first = pltpu.roll(taps_ref[...], 0, 1, stride=5, stride_axis=0)
+    taps = jnp.broadcast_to(taps_ref[...], (8, taps_ref.shape[1]))
+    first = pltpu.roll(taps, 0, 1, stride=5, stride_axis=0)
     banded = jnp.concatenate(
         [pltpu.roll(first, 40 * q, 1)[:, :384] for q in range(window // 8)], axis=0
     ).astype(jnp.bfloat16)[:, :rows]
@@ -181,7 +180,7 @@
     for d in range(bands):
         listed = jnp.int32(0)
         for s in range(bands):
-            hit = (dist_ref[0, s] == d + 1) & (s < count_ref[0])
+            hit = (plan_ref[s] == d + 1) & (s < plan_ref[2 * bands])
             listed = listed + hit.astype(jnp.int32)
         info = jnp.where(line == core * mine + d, listed.astype(jnp.float32), info)
     both[:, :, hc:] = jnp.broadcast_to(info[None], (n, 2 * mine, 128)).astype(jnp.bfloat16)
@@ -297,7 +296,7 @@
         chosen = jnp.zeros((share, block), jnp.float32)
         for d in range(bands):
             h, at = divmod(d * block, hb)
-            owned = (owner_ref[d] == to).astype(jnp.float32)
+            owned = (plan_ref[bands + d] == to).astype(jnp.float32)
             chosen = chosen + total[h * share : (h + 1) * share, at : at + block] * owned
         send3[to] = chosen
     for k in range(1, n):
@@ -329,21 +328,20 @@
     lanes = 1024
     start = lanes - 5 * lead - half
     line = jnp.pad(taps.astype(jnp.float32), (start, lanes - start - width))
-    line = jnp.broadcast_to(line[None], (8, lanes))
+    line = line[None]
+    plan = jnp.concatenate([tile_dist[0], owner, tile_count])
     vmem, hbm = pl.BlockSpec(memory_space=pltpu.VMEM), pl.BlockSpec(memory_space=pltpu.HBM)
     share = block // n
     sems = [pltpu.SemaphoreType.DMA((n,)) for _ in range(6)]
     return pl.pallas_call(
         functools.partial(fused_kernel, n, width, bands),
         out_shape=jax.ShapeDtypeStruct((1, block, block), jnp.float32),
-        in_specs=[hbm, hbm, hbm, hbm, vmem],
+        in_specs=[hbm, hbm, vmem],
         out_specs=vmem,
         scratch_shapes=[
-            pltpu.SMEM(tile_dist.shape, jnp.int32),
-            pltpu.SMEM(tile_count.shape, jnp.int32),
-            pltpu.SMEM(owner.shape, jnp.int32),
+            pltpu.SMEM(plan.shape, jnp.int32),
             pltpu.VMEM(raw.shape, raw.dtype),
-            pltpu.SemaphoreType.DMA((4,)),
+            pltpu.SemaphoreType.DMA((2,)),
             pltpu.VMEM((n, 2 * mine, channels // 2 + 128), jnp.bfloat16),
             pltpu.VMEM((n // 2, 2 * mine, channels // 2 + 128), jnp.bfloat16),
             pltpu.VMEM((n // 2, 2 * mine, channels // 2 + 128), jnp.bfloat16),
@@ -360,9 +358,9 @@
             *sems,
         ],
         compiler_params=pltpu.CompilerParams(
-            collective_id=0, has_side_effects=True, vmem_limit_bytes=61 * 2**20
+            collective_id=0, has_side_effects=True, vmem_limit_bytes=int(53.25 * 2**20)
         ),
-    )(tile_dist, tile_count, owner, raw, line)
+    )(plan, raw, line)
 
 
 def shards(raw, taps, tile_dist, tile_count, owner):

time: 30.4 us -> 28.2 us (0.928)
  local copies, waits for them, and re-layouts: 2.09 us -> 0.63 us
  Pallas kernels: 26.6 us -> 25.2 us
  other arithmetic: 0.73 us -> 1.48 us
    pallas_call x1, Pallas kernels: 26.6 us -> 25.2 us  [fused(): pl.pallas_call(functools.partial(fused_kernel, n, width, bands), out_shap...]
    unnamed x1, local copies, waits for them, and re-layouts: 1.47 us -> 0.63 us
    concatenate x0 -> x1, other arithmetic: none -> 0.75 us  [fused(): plan = jnp.concatenate([tile_dist[0], owner, tile_count])]
    broadcast_in_dim x0 -> x1, other arithmetic: none -> 0.73 us  [fused(): line = line[None]]
    pad x1 -> x0, other arithmetic: 0.73 us -> none  [fused(): line = jnp.pad(taps.astype(jnp.float32), (start, lanes - start - width))]
    broadcast_in_dim x1 -> x0, local copies, waits for them, and re-layouts: 0.62 us -> none  [fused(): line = jnp.broadcast_to(line[None], (8, lanes))]
where the time goes in v5:
time: 28.2 us; the launch traced here: 28 us
  Pallas kernels  25.2 us (89%)
  other arithmetic  1.48 us (5%)
  between operations  0.66 us (2%)
  local copies, waits for them, and re-layouts  0.63 us (2%)
    pallas_call x1, Pallas kernels, fused(): pl.pallas_call(functools.partial(fused_kernel, n, width, bands), out_shap...  25.2 us
    concatenate x1, other arithmetic, fused(): plan = jnp.concatenate([tile_dist[0], owner, tile_count])  0.75 us
    broadcast_in_dim x1, other arithmetic, fused(): line = line[None]  0.73 us
    unnamed x1, local copies, waits for them, and re-layouts  0.63 us

profile of v5, /device:TPU:0, one launch (start us, length us, event | category | flops | bytes accessed | tf_op | source)
XLA Modules:
  0.0 28.0 jit_solution(655621986947479351)
XLA Ops:
  0.7 0.7 %pad_add_fusion.plan_hbm = s32[9]{0:T(128)S(1)} fusion(s32[1]{0:T(128)S(6)} %copy.7, s32[4]{0:T(128)} %param.9, s32[4]{0:T(128)} %bitcast.3), kind=kLoop, calls=%fused_computation.1 | loop fusion | flops 18 | bytes 72 | tf_op jit(solution)/shard_map/concatenate | solution.py:332
  1.4 0.7 %pad_convert_fusion = f32[1024]{0:T(1024)S(1)} fusion(bf16[255]{0:T(256)(128)(2,1)} %param.6), kind=kLoop, calls=%fused_computation | loop fusion | flops 1024 | bytes 4606 | tf_op jit(solution)/shard_map/broadcast_in_dim | solution.py:331
  2.1 25.2 %shard_map.55 = f32[1,128,128]{2,1,0:T(8,128)S(1)} custom-call(s32[9]{0:T(128)S(1)} %pad_add_fusion.plan_hbm, bf16[320,2048]{1,0:T(8,128)(2,1)} %raw_hbm.1, f32[1,1024]{1,0:T(1,128)S(1)} %bitcast.2), custom_call_target="tpu_custom_call" | custom-call | tf_op jit(solution)/shard_map/pallas_call | solution.py:336
  27.4 0.6 %copy.8 = f32[1,128,128]{2,1,0:T(8,128)} copy(f32[1,128,128]{2,1,0:T(8,128)S(1)} %shard_map.55) | data formatting | bytes 131072
